TPU v7x, 32 devices: a whole 2x2x4 slice. The times are simulated.
32 devices in a mesh: dp: 16 (over z, y, core), mp: 2 (over x).
Axes of the slice: x: 2, y: 2, z: 4, core: 2. Of those that a mesh axis runs over, the one named last changes fastest.
Arguments:
- residual_in: bfloat16 [8192, 1024], P(('dp', 'mp')), may hold values from -6 to 6
- cotangent: bfloat16 [8192, 1024], P(('dp', 'mp')), may hold values from -6 to 6
- ln_gain: float32 [1024], replicated, may hold values from 0.5 to 1.5
- ln_bias: float32 [1024], replicated, may hold values from -3 to 3
- w_qkv: bfloat16 [3, 1024, 1024], P(None, 'dp', 'mp'), may hold values from -0.1875 to 0.1875
- w_out: bfloat16 [1024, 1024], P('mp', 'dp'), may hold values from -1.5 to 1.5
- w_in: bfloat16 [1024, 4096], P('dp', 'mp'), may hold values from -0.1875 to 0.1875
- b_in: bfloat16 [4096], P(('mp', 'dp')), may hold values from -3 to 3
- w_back: bfloat16 [4096, 1024], P('mp', 'dp'), may hold values from -0.09375 to 0.09375
- b_back: float32 [1024], replicated, may hold values from -3 to 3
- bucket_ids: int32 [16], P('dp'), may hold values from 0 to 3, as said below
- residue_counts: int32 [16, 16], P('dp'), may hold values from 30 to 256
Outputs:
- block_out: bfloat16 [8192, 1024], P(('dp', 'mp'))
- grad_input: bfloat16 [8192, 1024], P(('dp', 'mp'))
- grad_ln_gain: float32 [1024], P(('dp', 'mp'))
- grad_ln_bias: float32 [1024], P(('dp', 'mp'))
- grad_w_qkv: float32 [3, 1024, 1024], P(None, 'dp', 'mp')
- grad_w_out: float32 [1024, 1024], P('mp', 'dp')
- grad_w_in: float32 [1024, 4096], P('dp', 'mp')
- grad_b_in: float32 [4096], P(('mp', 'dp'))
- grad_w_back: float32 [4096, 1024], P('mp', 'dp')
- grad_b_back: float32 [1024], P(('dp', 'mp'))
Inputs may be any that keep to these rules, and one draw needn't show every extreme that they name: `bucket_ids`: every bucket number is held by the same number of groups.
All inputs are finite; a program needn't handle non-finite values.
Results may differ from a plain program's by a relative error of at most 0.017.
Values may be sent and summed in bfloat16 or wider, within the bound.
A program may use at most 192 MiB of HBM per device.

v0:
```python
from functools import partial

import jax
import jax.numpy as jnp
import numpy as np
from jax import lax
from jax.experimental import pallas as pl
from jax.experimental.pallas import tpu as pltpu
from jax.sharding import PartitionSpec as P

HD = 64
ROT = 32
SLOTS = 16


NORM_EPS = 1e-05
MASKED_SCORE = -1e30


def norm_rows(inputs_now, norm_gain, norm_shift):
    centred = inputs_now - jnp.mean(inputs_now, axis=-1, keepdims=True)
    spread = jnp.mean(centred * centred, axis=-1, keepdims=True)
    return centred * lax.rsqrt(spread + NORM_EPS) * norm_gain + norm_shift


def slot_tables(bucket_one, residue_row, group_rows):
    slot_length = jnp.right_shift(jnp.int32(group_rows // 2), bucket_one)
    places = jnp.arange(group_rows, dtype=jnp.int32)
    slot_ids = places // slot_length
    inside = places - slot_ids * slot_length
    match_table = slot_ids[:, None] == jnp.arange(SLOTS, dtype=jnp.int32)[None, :]
    picked = jnp.sum(jnp.where(match_table, residue_row[None, :], 0), axis=1)
    live_rows = jnp.minimum(picked, slot_length)
    return (slot_ids, inside, inside < live_rows)


def rope_tables(inside):
    half_steps = jnp.arange(ROT // 2, dtype=jnp.float32)
    inverse_rates = 10000.0 ** (-2.0 * half_steps / ROT)
    angles = inside.astype(jnp.float32)[:, None] * inverse_rates[None, :]
    return (jnp.cos(angles), jnp.sin(angles))


def rotate(values, cosine_table, sine_table):
    row_count = values.shape[0]
    head_count = values.shape[1]
    paired = values[..., :ROT].reshape(row_count, head_count, ROT // 2, 2)
    even_part = paired[..., 0]
    odd_part = paired[..., 1]
    cosine_now = cosine_table[:, None, :]
    sine_now = sine_table[:, None, :]
    turned = jnp.stack(
        [
            even_part * cosine_now - odd_part * sine_now,
            odd_part * cosine_now + even_part * sine_now,
        ],
        axis=-1,
    )
    return jnp.concatenate([turned.reshape(row_count, head_count, ROT), values[..., ROT:]], axis=-1)


def mask_block(block_start, block_rows, slot_ids):
    query_places = block_start + jnp.arange(block_rows, dtype=jnp.int32)
    query_slots = lax.dynamic_slice_in_dim(slot_ids, block_start, block_rows, 0)
    key_places = jnp.arange(slot_ids.shape[0], dtype=jnp.int32)
    return (query_slots[:, None] == slot_ids[None, :]) & (
        key_places[None, :] <= query_places[:, None]
    )


def over_rows(first_op, second_op):
    return lax.dot_general(
        first_op, second_op, (((0,), (0,)), ((), ())), preferred_element_type=jnp.float32
    )


def against_weight(first_op, second_op):
    return lax.dot_general(
        first_op, second_op, (((1,), (1,)), ((), ())), preferred_element_type=jnp.float32
    )


def on_device(
    residual_in,
    cotangent,
    ln_gain,
    ln_bias,
    w_qkv,
    w_out,
    w_in,
    b_in,
    w_back,
    b_back,
    bucket_ids,
    residue_counts,
):
    model_count = lax.axis_size("mp")
    model_rank = lax.axis_index("mp")
    local_rows = residual_in.shape[0]
    group_rows = local_rows * model_count
    slot_ids, inside, valid_rows = slot_tables(bucket_ids[0], residue_counts[0], group_rows)
    cosine_table, sine_table = rope_tables(inside)
    qkv_all, out_all, in_all, bias_in, back_all = (
        lax.all_gather(w_qkv, "dp", axis=1, tiled=True),
        lax.all_gather(w_out, "dp", axis=1, tiled=True),
        lax.all_gather(w_in, "dp", axis=0, tiled=True),
        lax.all_gather(b_in, "dp", axis=0, tiled=True),
        lax.all_gather(w_back, "dp", axis=1, tiled=True),
    )
    x_local = residual_in.astype(jnp.float32)
    x_group = lax.all_gather(residual_in, "mp", axis=0, tiled=True).astype(jnp.float32)
    normed = norm_rows(x_group, ln_gain, ln_bias).astype(jnp.bfloat16)
    head_width = qkv_all.shape[2]
    head_count = head_width // HD
    score_scale = HD ** (-0.5)

    def project(member_index):
        return jnp.dot(normed, qkv_all[member_index], preferred_element_type=jnp.float32).reshape(
            group_rows, head_count, HD
        )

    queries = rotate(project(0), cosine_table, sine_table).astype(jnp.bfloat16)
    key_rows = rotate(project(1), cosine_table, sine_table).astype(jnp.bfloat16)
    value_rows = project(2).astype(jnp.bfloat16)
    block_rows = min(512, group_rows)
    starts = jnp.arange(group_rows // block_rows, dtype=jnp.int32) * block_rows

    def block_scores(block_start):
        query_block = lax.dynamic_slice_in_dim(queries, block_start, block_rows, 0)
        allowed = mask_block(block_start, block_rows, slot_ids)
        scores = (
            jnp.einsum("qhd,khd->hqk", query_block, key_rows, preferred_element_type=jnp.float32)
            * score_scale
        )
        return (query_block, jnp.where(allowed[None], scores, MASKED_SCORE))

    def forward_block(block_start):
        query_block, scores = block_scores(block_start)
        row_peak = jnp.max(scores, axis=-1, keepdims=True)
        exp_scores = jnp.exp(scores - row_peak)
        row_total = jnp.sum(exp_scores, axis=-1, keepdims=True)
        weights_now = (exp_scores / row_total).astype(jnp.bfloat16)
        attended = jnp.einsum(
            "hqk,khd->qhd", weights_now, value_rows, preferred_element_type=jnp.float32
        )
        return (attended.astype(jnp.bfloat16), (row_peak + jnp.log(row_total))[..., 0])

    attended_blocks, log_totals = lax.map(forward_block, starts)
    mixed_rows = attended_blocks.reshape(group_rows, head_width)
    hidden = jnp.dot(normed, in_all, preferred_element_type=jnp.float32) + bias_in.astype(
        jnp.float32
    )
    gelu_tanh = partial(jax.nn.gelu, approximate=True)
    active_value, gelu_pull = jax.vjp(gelu_tanh, hidden)
    active = active_value.astype(jnp.bfloat16)
    partial_out = jnp.dot(mixed_rows, out_all, preferred_element_type=jnp.float32) + jnp.dot(
        active, back_all, preferred_element_type=jnp.float32
    )
    summed_all = lax.psum(partial_out.astype(jnp.bfloat16), "mp").astype(jnp.float32)
    summed = lax.dynamic_slice_in_dim(summed_all, model_rank * local_rows, local_rows, 0)
    block_out = (x_local + summed + b_back).astype(jnp.bfloat16)
    cot_group = lax.all_gather(cotangent, "mp", axis=0, tiled=True)
    seed_rows = jnp.where(valid_rows[:, None], cot_group, jnp.zeros_like(cot_group))
    qkv_all, out_all, in_all, back_all = (
        lax.all_gather(w_qkv, "dp", axis=1, tiled=True),
        lax.all_gather(w_out, "dp", axis=1, tiled=True),
        lax.all_gather(w_in, "dp", axis=0, tiled=True),
        lax.all_gather(w_back, "dp", axis=1, tiled=True),
    )
    active_grad = against_weight(seed_rows, back_all)
    hidden_grad = gelu_pull(active_grad)[0].astype(jnp.bfloat16)
    grad_in_local = over_rows(normed, hidden_grad)
    grad_bias_in = jnp.sum(hidden_grad.astype(jnp.float32), axis=0)
    grad_back_local = over_rows(active, seed_rows)
    grad_out_local = over_rows(mixed_rows, seed_rows)
    normed_grad = against_weight(hidden_grad, in_all)
    mixed_grad = (
        against_weight(seed_rows, out_all).astype(jnp.bfloat16).reshape(group_rows, head_count, HD)
    )

    def backward_block(carry, inputs_now):
        key_acc, value_acc = carry
        block_start, log_total = inputs_now
        query_block, scores = block_scores(block_start)
        grad_block = lax.dynamic_slice_in_dim(mixed_grad, block_start, block_rows, 0)
        probs = jnp.exp(scores - log_total[..., None])
        probs_low = probs.astype(jnp.bfloat16)
        value_acc = value_acc + jnp.einsum(
            "hqk,qhd->khd", probs_low, grad_block, preferred_element_type=jnp.float32
        )
        probs_grad = jnp.einsum(
            "qhd,khd->hqk", grad_block, value_rows, preferred_element_type=jnp.float32
        )
        score_grad = probs * (probs_grad - jnp.sum(probs * probs_grad, axis=-1, keepdims=True))
        score_low = score_grad.astype(jnp.bfloat16)
        query_grad = (
            jnp.einsum("hqk,khd->qhd", score_low, key_rows, preferred_element_type=jnp.float32)
            * score_scale
        )
        key_acc = (
            key_acc
            + jnp.einsum("hqk,qhd->khd", score_low, query_block, preferred_element_type=jnp.float32)
            * score_scale
        )
        return ((key_acc, value_acc), query_grad)

    empty_heads = jnp.zeros((group_rows, head_count, HD), jnp.float32)
    (key_acc, value_acc), query_blocks = lax.scan(
        backward_block, (empty_heads, empty_heads), (starts, log_totals)
    )
    turn_back = partial(rotate, cosine_table=cosine_table, sine_table=sine_table)
    unturn = jax.vjp(turn_back, empty_heads)[1]
    query_pre_grad = (
        unturn(query_blocks.reshape(group_rows, head_count, HD))[0]
        .astype(jnp.bfloat16)
        .reshape(group_rows, head_width)
    )
    key_pre_grad = unturn(key_acc)[0].astype(jnp.bfloat16).reshape(group_rows, head_width)
    value_grad = value_acc.astype(jnp.bfloat16).reshape(group_rows, head_width)
    grad_qkv_local = jnp.stack(
        [
            over_rows(normed, query_pre_grad),
            over_rows(normed, key_pre_grad),
            over_rows(normed, value_grad),
        ],
        axis=0,
    )
    normed_grad = (
        normed_grad
        + against_weight(query_pre_grad, qkv_all[0])
        + against_weight(key_pre_grad, qkv_all[1])
        + against_weight(value_grad, qkv_all[2])
    )
    share_grad = lax.psum(normed_grad.astype(jnp.bfloat16), "mp").astype(jnp.float32)
    seed_group = seed_rows.astype(jnp.float32)
    norm_pull = jax.vjp(norm_rows, x_group, ln_gain, ln_bias)[1]
    input_part, gain_part, shift_part = norm_pull(share_grad)
    input_group = seed_group + input_part
    grad_input = lax.dynamic_slice_in_dim(
        input_group, model_rank * local_rows, local_rows, 0
    ).astype(jnp.bfloat16)
    back_part = jnp.sum(seed_group, axis=0)
    grad_w_qkv, grad_w_out, grad_w_in, grad_b_in, grad_w_back, gain_rows, shift_rows, back_rows = (
        lax.psum_scatter(
            grad_qkv_local.astype(jnp.bfloat16), "dp", scatter_dimension=1, tiled=True
        ).astype(jnp.float32),
        lax.psum_scatter(
            grad_out_local.astype(jnp.bfloat16), "dp", scatter_dimension=1, tiled=True
        ).astype(jnp.float32),
        lax.psum_scatter(
            grad_in_local.astype(jnp.bfloat16), "dp", scatter_dimension=0, tiled=True
        ).astype(jnp.float32),
        lax.psum_scatter(
            grad_bias_in.astype(jnp.bfloat16), "dp", scatter_dimension=0, tiled=True
        ).astype(jnp.float32),
        lax.psum_scatter(
            grad_back_local.astype(jnp.bfloat16), "dp", scatter_dimension=1, tiled=True
        ).astype(jnp.float32),
        lax.psum_scatter(
            gain_part.astype(jnp.bfloat16), "dp", scatter_dimension=0, tiled=True
        ).astype(jnp.float32),
        lax.psum_scatter(
            shift_part.astype(jnp.bfloat16), "dp", scatter_dimension=0, tiled=True
        ).astype(jnp.float32),
        lax.psum_scatter(
            back_part.astype(jnp.bfloat16), "dp", scatter_dimension=0, tiled=True
        ).astype(jnp.float32),
    )
    piece_width = gain_rows.shape[0] // model_count
    grad_ln_gain = lax.dynamic_slice_in_dim(gain_rows, model_rank * piece_width, piece_width, 0)
    grad_ln_bias = lax.dynamic_slice_in_dim(shift_rows, model_rank * piece_width, piece_width, 0)
    grad_b_back = lax.dynamic_slice_in_dim(back_rows, model_rank * piece_width, piece_width, 0)
    return (
        block_out,
        grad_input,
        grad_ln_gain,
        grad_ln_bias,
        grad_w_qkv,
        grad_w_out,
        grad_w_in,
        grad_b_in,
        grad_w_back,
        grad_b_back,
    )


MESH = pl.DeviceIdType.MESH
NZ = 4
TILE = 256
N_HEADS = TILE // HD
NQ = 4
NJ = 4
NK = NQ + 2 * NJ
VROWS = 56


def fits_quad(mesh):
    return mesh.shape["mp"] == 2 and mesh.shape["dp"] == 4 * NZ


def dot_nn(a, b):
    return lax.dot_general(a, b, (((1,), (0,)), ((), ())), preferred_element_type=jnp.float32)


def dot_nt(a, b):
    return lax.dot_general(a, b, (((1,), (1,)), ((), ())), preferred_element_type=jnp.float32)


def dot_tn(a, b):
    return lax.dot_general(a, b, (((0,), (0,)), ((), ())), preferred_element_type=jnp.float32)


def layer_kernel(
    bucket_ref,
    counts_ref,
    x_ref,
    cot_ref,
    gain_ref,
    bias_ref,
    bback_ref,
    cos_ref,
    sin_ref,
    bin_ref,
    wqkv_ref,
    wot_ref,
    win_ref,
    wbt_ref,
    block_ref,
    gin_ref,
    gqkv_ref,
    got_ref,
    gi_ref,
    gbt_ref,
    lng_ref,
    lnb_ref,
    bbk_ref,
    gbin_ref,
    B,
    W,
    NS,
    CT,
    SN,
    BM,
    QR,
    KR,
    VR,
    R,
    XV,
    CV,
    COSV,
    SINV,
    ins,
    OUT,
    DN,
    GP,
    GC,
    RZ,
    FS,
    YS,
    YR,
    XH,
    RSTD,
    EXSa,
    EXSb,
    EYSa,
    EYSb,
    EXRa,
    EXRb,
    EYRa,
    EYRb,
    EXS2a,
    EXS2b,
    EYS2a,
    EYS2b,
    EXR2a,
    EXR2b,
    EYR2a,
    EYR2b,
    V,
    VS,
    VRV,
    loc_sem,
    ays,
    ayr,
    azs,
    azr,
    acs,
    acr,
    gs,
    gr,
    rcs,
    rcr,
    rzs,
    rzr,
    rys,
    ryr,
    exs,
    exr,
    vs,
    vr,
):
    EXS = (EXSa, EXSb)
    EYS = (EYSa, EYSb)
    EXR = (EXRa, EXRb)
    EYR = (EYRa, EYRb)
    EXS2 = (EXS2a, EXS2b)
    EYS2 = (EYS2a, EYS2b)
    EXR2 = (EXR2a, EXR2b)
    EYR2 = (EYR2a, EYR2b)
    f32, bf16 = jnp.float32, jnp.bfloat16
    dp, x = lax.axis_index("dp"), lax.axis_index("mp")
    z = dp // 4
    y = lax.rem(dp // 2, 2)
    c = lax.rem(dp, 2)
    rows = x_ref.shape[0]
    width = x_ref.shape[1]
    dev_x = (dp, 1 - x)
    dev_y = (dp + 2 - 4 * y, x)
    dev_c = (dp + 1 - 2 * c, x)
    dev_r = (lax.rem(dp + 4, 4 * NZ), x)
    dev_l = (lax.rem(dp + 4 * NZ - 4, 4 * NZ), x)
    dev_z = [(lax.rem(dp + 4 * i, 4 * NZ), x) for i in (1, 2, 3)]
    NA, SA = NS.at[0], NS.at[1]
    m_own = 2 * y + x
    m_x = 2 * y + 1 - x
    m_y = 2 - 2 * y + x
    m_d = 3 - m_own

    def rcp(src, dst, ss, rs, dev):
        return pltpu.make_async_remote_copy(
            src_ref=src, dst_ref=dst, send_sem=ss, recv_sem=rs, device_id=dev, device_id_type=MESH
        )

    barrier = pltpu.get_barrier_semaphore()
    peers = [dev_x, dev_y, dev_c] + dev_z
    for peer in peers:
        pl.semaphore_signal(barrier, inc=1, device_id=peer, device_id_type=MESH)

    def wsrc(k, q):
        if k == NK:
            return None
        if k < 3:
            return wqkv_ref.at[k, :, pl.ds(pl.multiple_of(q * TILE, TILE), TILE)]
        if k == 3:
            return wot_ref.at[:, pl.ds(pl.multiple_of(q * TILE, TILE), TILE)]
        ref = win_ref if k % 2 == 0 else wbt_ref
        j = (k - NQ) // 2
        return ref.at[:, pl.ds(pl.multiple_of(q * (NJ * TILE) + j * TILE, TILE), TILE)]

    def wv(k):
        return B if isinstance(k, int) and k == NK else W.at[k]

    def own_copy(k):
        return pltpu.make_async_copy(wsrc(k, y), W.at[k, z, y, c], loc_sem.at[k])

    def y_copy(k):
        if k == NK:
            return rcp(B.at[z, y, c], B.at[z, y, c], ays.at[k], ayr.at[k], dev_y)
        return rcp(wsrc(k, 1 - y), W.at[k, z, y, c], ays.at[k], ayr.at[k], dev_y)

    def y_arrived(k):
        here = wv(k).at[z, 1 - y, c]
        rcp(here, here, ays.at[k], ayr.at[k], dev_y).wait_recv()

    def z_copy(k, way, s, e):
        block = wv(k).at[e, :, c]
        return rcp(
            block, block, azs.at[k, way, s], azr.at[k, way, s], dev_r if way == 0 else dev_l
        )

    def c_copy(k, e):
        block = wv(k).at[e, :, c]
        return rcp(block, block, acs.at[k, e], acr.at[k, e], dev_c)

    def ag_own(k, copied=True):
        if copied:
            pltpu.make_async_copy(
                W.at[k, z, y, c], W.at[k, z, y, c], loc_sem.at[k]
            ).wait()
        y_arrived(k)

        @pl.when(z < NZ - 1)
        def _():
            z_copy(k, 0, 0, z).start()

        @pl.when(z > 0)
        def _():
            z_copy(k, 1, 0, z).start()

        c_copy(k, z).start()

    def ag_step(k, s):
        @pl.when(z - 1 - s >= 0)
        def _():
            e = z - 1 - s
            z_copy(k, 0, s, e).wait_recv()
            if s < NZ - 2:

                @pl.when(z < NZ - 1)
                def _():
                    z_copy(k, 0, s + 1, e).start()

            c_copy(k, e).start()

        @pl.when(z + 1 + s <= NZ - 1)
        def _():
            e = z + 1 + s
            z_copy(k, 1, s, e).wait_recv()
            if s < NZ - 2:

                @pl.when(z > 0)
                def _():
                    z_copy(k, 1, s + 1, e).start()

            c_copy(k, e).start()

    def ag_done(k):
        for e in range(NZ):
            block = wv(k).at[e, :, 1 - c]
            rcp(block, block, acs.at[k, e], acr.at[k, e], dev_c).wait_recv()

    def ag_sent(k, copied=True):
        y_copy(k).wait_send() if isinstance(k, int) else None
        for s in range(NZ - 1):

            @pl.when((z < NZ - 1) & (z - s >= 0))
            def _():
                z_copy(k, 0, s, z - s).wait_send()

            @pl.when((z > 0) & (z + s <= NZ - 1))
            def _():
                z_copy(k, 1, s, z + s).wait_send()

        for e in range(NZ):
            c_copy(k, e).wait_send()

    order = [0, NK] + list(range(1, NK))
    turns = iter([t for t in range(NK + NZ) if not 8 <= t <= 11])

    def ag_turn():
        t = next(turns, None)
        if t is None:
            return
        for n in range(2) if t == 0 else (t + 1,):
            if n <= NK:
                ag_own(order[n], copied=order[n] != NK)
        for s in range(NZ - 1):
            if 0 <= t - 1 - s <= NK:
                ag_step(order[t - 1 - s], s)

    def late_turn(t):
        ag_own(t)
        for s in range(NZ - 1):
            ag_step(t - 2 - s, s)

    P0 = 80
    parts = (pl.ds(0, P0), pl.ds(P0, rows - P0))
    BUF = (NA, SA)

    def g_copy(t, p, way, m):
        block = BUF[t].at[m, parts[p]]
        i = (t * 2 + p) * 3 + way
        dev = (dev_x, dev_y)[way] if way < 2 else (dev_y, dev_x)[p]
        return rcp(block, block, gs.at[i], gr.at[i], dev)

    def g_send(t):
        g_copy(t, 0, 0, m_own).start()
        g_copy(t, 1, 1, m_own).start()
        g_copy(t, 1, 0, m_own).start()
        g_copy(t, 0, 1, m_own).start()

    def g_near(t):
        g_copy(t, 0, 0, m_x).wait_recv()
        g_copy(t, 1, 1, m_y).wait_recv()

    def g_forward(t):
        g_copy(t, 0, 2, m_x).start()
        g_copy(t, 1, 2, m_y).start()

    def g_rest(t):
        g_copy(t, 1, 0, m_x).wait_recv()
        g_copy(t, 0, 1, m_y).wait_recv()

    def g_far(t):
        g_copy(t, 0, 2, m_d).wait_recv()
        g_copy(t, 1, 2, m_d).wait_recv()

    def g_sent(t):
        for p in (0, 1):
            for way in (0, 1):
                g_copy(t, p, way, m_own).wait_send()
        g_copy(t, 0, 2, m_x).wait_send()
        g_copy(t, 1, 2, m_y).wait_send()

    def rs_c(k):
        return rcp(GP.at[k, :, :, 1 - c], GC.at[k], rcs.at[k], rcr.at[k], dev_c)

    def rs_z(k, way, e, slot):
        return rcp(
            GP.at[k, e, :, c],
            RZ.at[k, slot],
            rzs.at[k, e],
            rzr.at[k, slot],
            dev_r if way == 0 else dev_l,
        )

    def rs_begin(k):
        rs_c(k).wait_recv()
        for e in range(NZ):
            GP[k, e, :, c] = (GP[k, e, :, c].astype(f32) + GC[k, e].astype(f32)).astype(bf16)

        @pl.when(z == 0)
        def _():
            for e in range(NZ - 1, 0, -1):
                rs_z(k, 0, e, e).start()

        @pl.when(z == NZ - 1)
        def _():
            for e in range(NZ - 1):
                rs_z(k, 1, e, e if e < NZ - 2 else 4).start()

    def pass_on(k, way, e, slot):
        rs_z(k, way, e, e).wait_recv()
        GP[k, e, :, c] = (GP[k, e, :, c].astype(f32) + RZ[k, e].astype(f32)).astype(bf16)
        rs_z(k, way, e, slot).start()

    def rs_hop1(k):
        @pl.when(z == 1)
        def _():
            pass_on(k, 0, 3, 3)
            pass_on(k, 0, 2, 2)

        @pl.when(z == 2)
        def _():
            pass_on(k, 1, 0, 0)
            pass_on(k, 1, 1, 4)

    def rs_hop2(k):
        @pl.when(z == 2)
        def _():
            pass_on(k, 0, 3, 3)

        @pl.when(z == 1)
        def _():
            pass_on(k, 1, 0, 4)

    def rs_y(k):
        return rcp(YS.at[k], YR.at[k], rys.at[k], ryr.at[k], dev_y)

    def put(k, q, value):
        if k < 3:
            gqkv_ref[k, :, pl.ds(pl.multiple_of(q * TILE, TILE), TILE)] = value
        elif k == 3:
            got_ref[:, pl.ds(pl.multiple_of(q * TILE, TILE), TILE)] = value
        else:
            ref = gi_ref if k % 2 == 0 else gbt_ref
            j = (k - NQ) // 2
            ref[:, pl.ds(pl.multiple_of(q * (NJ * TILE) + j * TILE, TILE), TILE)] = value

    def rs_final(k):
        FS[...] = GP[k, z, :, c].astype(f32)

        @pl.when(z > 0)
        def _():
            rs_z(k, 0, z, z).wait_recv()
            FS[...] += RZ[k, z].astype(f32)

        @pl.when(z < NZ - 1)
        def _():
            rs_z(k, 1, z, 4).wait_recv()
            FS[...] += RZ[k, 4].astype(f32)

        YS[k] = FS[1 - y].astype(bf16)
        rs_y(k).start()
        put(k, y, FS[y])

    def rs_out(k):
        rs_y(k).wait_recv()
        put(k, 1 - y, YR[k].astype(f32))

    rturns = iter(range(NK + 2))

    def rs_turn():
        r = next(rturns, None)
        if r is None:
            return
        for s, f in enumerate((rs_hop1, rs_hop2, rs_final)):
            if 0 <= r - s < NK:
                f(r - s)

    def rs_sent(k):
        rs_c(k).wait_send()
        for e in range(NZ):

            @pl.when(z != e)
            def _():
                rs_z(k, 0, e, e).wait_send()

        rs_y(k).wait_send()

    def e_copy(t, u, i):
        src, dst, dev = (
            (EXS, EXR, dev_x),
            (EYS, EYR, dev_y),
            (EXS2, EXR2, dev_x),
            (EYS2, EYR2, dev_y),
        )[i]
        src, dst = src[u], dst[u]
        return rcp(src.at[t], dst.at[t], exs.at[t, u, i], exr.at[t, u, i], dev)

    wide = (384, 256)
    thin = (2 * 128, 128)

    def cols(u, half):
        if half == 0:
            return pl.ds(u * wide[0], wide[u])
        return pl.ds(sum(wide) + u * thin[0], thin[u])

    def e_first_x(t, u, P):
        for i in range(2):
            EXS[u][t, i] = P[2 * i + 1 - x, :, cols(u, 0)].astype(bf16)
        e_copy(t, u, 0).start()

    def e_first_y(t, u, P):
        for i in range(2):
            EYS[u][t, i] = P[2 - 2 * y + i, :, cols(u, 1)].astype(bf16)
        e_copy(t, u, 1).start()

    def e_first(t, u, P):
        e_first_x(t, u, P)
        e_first_y(t, u, P)

    def e_second(t, u, P):
        e_copy(t, u, 0).wait_recv()
        EYS2[u][t] = (P[m_y, :, cols(u, 0)] + EXR[u][t, 1 - y].astype(f32)).astype(bf16)
        e_copy(t, u, 3).start()
        e_copy(t, u, 1).wait_recv()
        EXS2[u][t] = (P[m_x, :, cols(u, 1)] + EYR[u][t, 1 - x].astype(f32)).astype(bf16)
        e_copy(t, u, 2).start()

    def e_last(t, u, P):
        e_copy(t, u, 3).wait_recv()
        P[m_own, :, cols(u, 0)] += EXR[u][t, y].astype(f32) + EYR2[u][t].astype(f32)
        e_copy(t, u, 2).wait_recv()
        P[m_own, :, cols(u, 1)] += EYR[u][t, x].astype(f32) + EXR2[u][t].astype(f32)

    def e_sent(t):
        for u in range(2):
            for i in range(4):
                e_copy(t, u, i).wait_send()

    inputs = [
        pltpu.make_async_copy(src, dst, ins.at[i])
        for i, (src, dst) in enumerate(
            ((x_ref, XV), (cot_ref, CV), (cos_ref, COSV), (sin_ref, SINV))
        )
    ]
    for copy in inputs:
        copy.start()
    for k in range(NK):
        own_copy(k).start()
    inputs[0].wait()
    xf = XV[...].astype(f32)
    centred = xf - jnp.mean(xf, axis=-1, keepdims=True)
    rstd = lax.rsqrt(jnp.mean(centred * centred, axis=-1, keepdims=True) + NORM_EPS)
    xhat = centred * rstd
    XH[...] = xhat
    RSTD[...] = jnp.broadcast_to(rstd, RSTD.shape)
    NA[m_own] = (xhat * gain_ref[...] + bias_ref[...]).astype(bf16)

    bucket = bucket_ref[0]
    B[z, y, c, 0:8] = jnp.broadcast_to(bin_ref[...].astype(f32), (8, 128)).astype(bf16)
    B[z, y, c, 8:16] = jnp.full((8, 128), bucket.astype(f32), f32).astype(bf16)

    slot = lax.shift_right_logical(jnp.int32(rows), bucket)
    shift_of = (rows.bit_length() - 1) - bucket
    row = x * rows + lax.broadcasted_iota(jnp.int32, (rows, 128), 0)
    slot_of = lax.shift_right_logical(row, jnp.full(row.shape, shift_of, jnp.int32))
    place = row & jnp.full(row.shape, slot - 1, jnp.int32)
    limit = jnp.zeros((rows, 128), jnp.int32)
    for s in range(SLOTS):
        limit = jnp.where(slot_of == s, counts_ref[s], limit)
    valid = jnp.where(place < limit, 1.0, 0.0)[:, 0:1]
    inputs[1].wait()
    seeds = CV[...].astype(f32) * valid
    SA[m_own] = seeds.astype(bf16)
    back_sum = jnp.sum(seeds, axis=0, keepdims=True)
    V[...] = jnp.zeros_like(V)
    for i in range(8):
        V[16 + i : 17 + i, :] = back_sum[:, i * 128 : (i + 1) * 128]
    pl.semaphore_wait(barrier, len(peers))
    for k in order:
        y_copy(k).start()
    g_send(0)
    g_send(1)
    ag_turn()
    ag_turn()

    lane = lax.broadcasted_iota(jnp.int32, (rows, TILE), 1)
    even = (lane & 1) == 0

    def table(g):
        brow = B[z, g, c].astype(f32)[8:9, :]
        ba = jnp.broadcast_to(brow, (rows, 128))

        def pick(ref):
            full = ref[...]
            out = full
            for b in range(1, 4):
                n = rows >> b
                out = jnp.where(ba == float(b), jnp.concatenate([full[:n]] * (1 << b), axis=0), out)
            return out

        cg, sg = pick(COSV), pick(SINV)
        CT[g] = jnp.concatenate([cg, cg], axis=1)
        SN[g] = jnp.concatenate([sg, sg], axis=1)
        size = jnp.full((rows, 128), rows, jnp.int32)
        for b in range(1, 4):
            size = jnp.where(ba == float(b), rows >> b, size)
        size = jnp.concatenate([size, size], axis=1)
        qi = lax.broadcasted_iota(jnp.int32, (rows, rows), 0)
        ki = lax.broadcasted_iota(jnp.int32, (rows, rows), 1)
        BM[g] = jnp.where((ki <= qi) & ((qi ^ ki) < size), 0.0, MASKED_SCORE)

    def tables():
        for g in range(2):
            table(g)

    def turn(v, g, sign):
        other = jnp.where(even, -pltpu.roll(v, TILE - 1, 1), pltpu.roll(v, 1, 1))
        return v * CT[g] + (sign * other) * SN[g]

    def weight(k):
        return W[k].reshape(width, TILE)

    scale = HD ** (-0.5)

    def project(m):
        g = m // 2
        nb = NA[m]
        QR[m] = turn(dot_nn(nb, weight(0)), g, 1.0).astype(bf16)
        KR[m] = turn(dot_nn(nb, weight(1)), g, 1.0).astype(bf16)
        VR[m] = dot_nn(nb, weight(2)).astype(bf16)

    def attend(m):
        g = m // 2
        q, kk, v = QR[m], KR[m], VR[m]
        da = dot_nn(SA[m], weight(3)).astype(bf16)
        zero = jnp.zeros((rows, TILE), bf16)
        ps, ss, qs, ks, vs_, ds = [], [], [], [], [], []
        for h in range(N_HEADS):
            mine = (lane // HD) == h
            qh, kh, vh, dh = (jnp.where(mine, t, zero) for t in (q, kk, v, da))
            s = dot_nt(qh, kk) * scale + BM[g]
            e = jnp.exp(s - jnp.max(s, axis=-1, keepdims=True))
            p = e * (1.0 / jnp.sum(e, axis=-1, keepdims=True))
            pg = dot_nt(dh, v)
            sg = p * (pg - jnp.sum(p * pg, axis=-1, keepdims=True))
            for held, t in ((ps, p), (ss, sg), (qs, qh), (ks, kh), (vs_, vh), (ds, dh)):
                held.append(t.astype(bf16))
        wide_p, wide_s = jnp.concatenate(ps, axis=1), jnp.concatenate(ss, axis=1)
        att = dot_nn(wide_p, jnp.concatenate(vs_, axis=0))
        dq = dot_nn(wide_s, jnp.concatenate(ks, axis=0))
        dk = dot_tn(jnp.concatenate(ss, axis=0), jnp.concatenate(qs, axis=0))
        dv = dot_tn(jnp.concatenate(ps, axis=0), jnp.concatenate(ds, axis=0))
        at = att.astype(bf16)
        dqb = turn(dq * scale, g, -1.0).astype(bf16)
        dkb = turn(dk * scale, g, -1.0).astype(bf16)
        dvb = dv.astype(bf16)
        rs = pl.ds(pl.multiple_of(m * rows, rows), rows)
        R[3, rs, :] = at
        R[0, rs, :] = dqb
        R[1, rs, :] = dkb
        R[2, rs, :] = dvb
        OUT[m] = dot_nt(at, weight(3))
        DN[m] = dot_nt(dqb, weight(0)) + dot_nt(dkb, weight(1)) + dot_nt(dvb, weight(2))

    def grad_of(k, left):
        total = dot_tn(NS[left].reshape(4 * rows, width), R[k])
        GP[k] = total.astype(bf16).reshape(NZ, 2, 2, 64, TILE)
        rs_c(k).start()

    def slice_of(j):
        return NQ + 2 * j, NQ + 1 + 2 * j

    def feed(j, m, count=1):
        ki, kb = slice_of(j)
        n = count * rows
        b0 = B[2 * y + lax.div(j, 2), lax.rem(j, 2), 0].astype(f32)[0:1, :]
        b1 = B[2 * y + lax.div(j, 2), lax.rem(j, 2), 1].astype(f32)[0:1, :]
        take = lambda ref: ref[pl.ds(m, count)].reshape(n, width)
        u = dot_nn(take(NA), weight(ki)) + jnp.concatenate([b0, b1], axis=1)
        u2 = u * u
        k0 = float(np.sqrt(2.0 / np.pi))
        t = jnp.tanh(k0 * u * (1.0 + 0.044715 * u2))
        act = (0.5 * u * (1.0 + t)).astype(bf16)
        slope = 0.5 * (1.0 + t) + (0.5 * k0) * u * (1.0 - t * t) * (1.0 + 0.134145 * u2)
        hg = (dot_nn(take(SA), weight(kb)) * slope).astype(bf16)
        rs = pl.ds(pl.multiple_of(m * rows, rows), n)
        R[kb, rs, :] = act
        R[ki, rs, :] = hg
        OUT[pl.ds(m, count)] += dot_nt(act, weight(kb)).reshape(count, rows, width)
        DN[pl.ds(m, count)] += dot_nt(hg, weight(ki)).reshape(count, rows, width)
        at = 24 + x * 16 + y * 8 + 2 * j
        total = jnp.sum(hg.astype(f32), axis=0, keepdims=True)
        V[pl.ds(at, 1), :] += total[:, :128]
        V[pl.ds(at + 1, 1), :] += total[:, 128:]

    def feed_grads(j):
        lax.fori_loop(0, 2, lambda i, _: (grad_of(NQ + 2 * j + i, i), 0)[1], 0)

    def v_copy(i, dev):
        return rcp(VS.at[min(i, 3)], VRV.at[i], vs.at[i], vr.at[i], dev)

    v_devs = (dev_c, dev_x, dev_y)

    def v_step(i):
        v_copy(i, v_devs[i]).wait_recv()
        VS[i + 1] = VS[i] + VRV[i]
        if i < 2:
            v_copy(i + 1, v_devs[i + 1]).start()
        else:
            for n, dev in enumerate(dev_z):
                v_copy(3 + n, dev).start()

    def arrived(*chunks):
        for k in chunks:
            ag_done(k)

    ag_turn()
    inputs[2].wait()
    inputs[3].wait()
    tables()
    ag_turn()
    ag_turn()
    ag_turn()
    g_near(0)
    g_forward(0)
    ag_turn()
    arrived(0, NK, 1, 2)
    g_rest(0)
    def near(i):
        ix, iy = lax.rem(i, 2), lax.div(i, 2)
        return 2 * (y + iy - 2 * y * iy) + x + ix - 2 * x * ix

    lax.fori_loop(0, 3, lambda i, _: (project(near(i)), 0)[1], 0)
    ag_turn()
    arrived(3)

    def rows_turn(i, _):
        @pl.when(i == 1)
        def _():
            g_near(1)
            g_forward(1)
            g_rest(1)

        @pl.when(i == 3)
        def _():
            g_far(0)
            project(m_d)
            g_far(1)

        attend(near(i))
        late_turn(8 + i)
        return 0

    lax.fori_loop(0, 4, rows_turn, 0)

    def head_grads(k, _):
        grad_of(k, lax.div(k, 3))

        @pl.when(k > 0)
        def _():
            rs_begin(k - 1)

        return 0

    lax.fori_loop(0, NQ, head_grads, 0)
    ag_turn()

    def slices(j, _):
        arrived(NQ + 2 * j, NQ + 1 + 2 * j)
        feed(j, 0, 4)

        @pl.when(j == 0)
        def _():
            rs_begin(3)
            ag_turn()
            rs_turn()

        @pl.when(j == 1)
        def _():
            ag_turn()
            feed_grads(0)
            rs_turn()
            rs_begin(4)

        @pl.when(j == 2)
        def _():
            rs_begin(5)
            ag_turn()
            rs_turn()

        return 0

    lax.fori_loop(0, NJ, slices, 0)

    for u in range(2):
        e_first(1, u, DN)
    rs_turn()
    feed_grads(1)
    rs_begin(6)
    rs_begin(7)
    rs_turn()
    feed_grads(2)
    rs_begin(8)
    rs_begin(9)
    rs_turn()
    e_second(1, 0, DN)
    e_first(0, 0, OUT)
    feed_grads(3)
    rs_begin(10)
    rs_begin(11)
    e_second(1, 1, DN)
    e_first_y(0, 1, OUT)
    rs_turn()
    rs_turn()
    rs_turn()
    rs_turn()
    for u in range(2):
        e_last(1, u, DN)
    dn = DN[m_own]
    xhat = XH[...]
    gsum = jnp.sum(dn * xhat, axis=0, keepdims=True)
    bsum = jnp.sum(dn, axis=0, keepdims=True)
    for i in range(8):
        V[i : i + 1, :] = gsum[:, i * 128 : (i + 1) * 128]
        V[8 + i : 9 + i, :] = bsum[:, i * 128 : (i + 1) * 128]
    VS[0] = V[...]
    v_copy(0, dev_c).start()
    e = dn * gain_ref[...]
    me = jnp.mean(e, axis=-1, keepdims=True)
    mex = jnp.mean(e * xhat, axis=-1, keepdims=True)
    gin_ref[...] = (SA[m_own].astype(f32) + RSTD[:, 0:1] * (e - me - xhat * mex)).astype(bf16)
    v_step(0)
    e_first_x(0, 1, OUT)
    e_second(0, 0, OUT)
    rs_turn()
    v_step(1)
    rs_turn()
    v_step(2)
    for k in range(6):
        rs_out(k)
    rs_turn()
    e_second(0, 1, OUT)
    rs_turn()
    for k in range(6, 9):
        rs_out(k)
    for k in range(9, NK):
        rs_out(k)
    for i in range(3):
        v_copy(3 + i, dev_z[i]).wait_recv()
    V[...] = VS[3] + VRV[3] + VRV[4] + VRV[5]
    index = 2 * dp + x
    lane4 = lax.rem(index, 4)
    for base, ref in ((0, lng_ref), (8, lnb_ref), (16, bbk_ref)):
        line = V[pl.ds(base + index // 4, 1), :]
        out = line[:, 0:32]
        for n in range(1, 4):
            out = jnp.where(lane4 == n, line[:, 32 * n : 32 * n + 32], out)
        ref[...] = out
    gbin_ref[...] = V[pl.ds(24 + 16 * x + dp, 1), :]
    for u in range(2):
        e_last(0, u, OUT)
    block_ref[...] = (XV[...].astype(f32) + OUT[m_own] + bback_ref[...]).astype(bf16)

    def later(f):
        lax.fori_loop(0, NK, lambda k, _: (f(k), 0)[1], 0)

    for k in range(NK + 1):
        ag_sent(k)
    for t in range(2):
        g_sent(t)
        e_sent(t)
    later(rs_sent)
    for i, dev in enumerate([dev_c, dev_x, dev_y] + dev_z):
        v_copy(i, dev).wait_send()


def write_kernel(*refs):
    srcs, dsts, sems = refs[:10], refs[10:20], refs[20]
    copies = [pltpu.make_async_copy(a, b, sems.at[i]) for i, (a, b) in enumerate(zip(srcs, dsts))]
    for copy in copies:
        copy.start()
    for copy in copies:
        copy.wait()


def rope_constants(rows):
    half = np.arange(ROT // 2, dtype=np.float32)
    rates = (10000.0 ** (-2.0 * half / ROT)).astype(np.float32)
    angle = np.arange(rows, dtype=np.float32)[:, None] * rates[None, :]
    angle = np.repeat(angle, 2, axis=1)
    cos = np.concatenate([np.cos(angle), np.ones((rows, HD - ROT))], axis=1)
    sin = np.concatenate([np.sin(angle), np.zeros((rows, HD - ROT))], axis=1)
    two = lambda t: np.concatenate([t, t], axis=1).astype(np.float32)
    return two(cos), two(sin)


def on_quad(
    residual_in,
    cotangent,
    ln_gain,
    ln_bias,
    w_qkv,
    w_out,
    w_in,
    b_in,
    w_back,
    b_back,
    bucket_ids,
    residue_counts,
):
    rows, width = residual_in.shape
    cos, sin = rope_constants(rows)
    f32, bf16 = jnp.float32, jnp.bfloat16
    vm = pl.BlockSpec(memory_space=pltpu.VMEM)
    sm = pl.BlockSpec(memory_space=pltpu.SMEM)
    anyspace = pl.BlockSpec(memory_space=pl.ANY)
    shard = width // (4 * NZ)
    sem = pltpu.SemaphoreType.DMA
    shapes = (
        jax.ShapeDtypeStruct((rows, width), bf16),
        jax.ShapeDtypeStruct((rows, width), bf16),
        jax.ShapeDtypeStruct((3, shard, 2 * TILE), f32),
        jax.ShapeDtypeStruct((shard, 2 * TILE), f32),
        jax.ShapeDtypeStruct((shard, 2 * NJ * TILE), f32),
        jax.ShapeDtypeStruct((shard, 2 * NJ * TILE), f32),
        jax.ShapeDtypeStruct((1, 32), f32),
        jax.ShapeDtypeStruct((1, 32), f32),
        jax.ShapeDtypeStruct((1, 32), f32),
        jax.ShapeDtypeStruct((1, 128), f32),
    )
    held = pl.pallas_call(
        layer_kernel,
        out_shape=tuple(pltpu.VMEM(v.shape, v.dtype) for v in shapes),
        in_specs=[sm, sm, anyspace, anyspace] + [vm] * 3 + [anyspace] * 2 + [vm] + [anyspace] * 4,
        out_specs=(vm,) * 10,
        scratch_shapes=[
            pltpu.VMEM((NZ, 2, 2, 16, 128), bf16),
            pltpu.VMEM((NK, NZ, 2, 2, shard, TILE), bf16),
            pltpu.VMEM((2, 4, rows, width), bf16),
            pltpu.VMEM((2, rows, TILE), f32),
            pltpu.VMEM((2, rows, TILE), f32),
            pltpu.VMEM((2, rows, rows), f32),
            pltpu.VMEM((4, rows, TILE), bf16),
            pltpu.VMEM((4, rows, TILE), bf16),
            pltpu.VMEM((4, rows, TILE), bf16),
            pltpu.VMEM((NK, 4 * rows, TILE), bf16),
            pltpu.VMEM((rows, width), bf16),
            pltpu.VMEM((rows, width), bf16),
            pltpu.VMEM((rows, 128), f32),
            pltpu.VMEM((rows, 128), f32),
            sem((4,)),
            pltpu.VMEM((4, rows, width), f32),
            pltpu.VMEM((4, rows, width), f32),
            pltpu.VMEM((NK, NZ, 2, 2, shard, TILE), bf16),
            pltpu.VMEM((NK, NZ, 2, shard, TILE), bf16),
            pltpu.VMEM((NK, 5, 2, shard, TILE), bf16),
            pltpu.VMEM((2, shard, TILE), f32),
            pltpu.VMEM((NK, shard, TILE), bf16),
            pltpu.VMEM((NK, shard, TILE), bf16),
            pltpu.VMEM((rows, width), f32),
            pltpu.VMEM((rows, 128), f32),
            pltpu.VMEM((2, 2, rows, 384), bf16),
            pltpu.VMEM((2, 2, rows, 256), bf16),
            pltpu.VMEM((2, 2, rows, 256), bf16),
            pltpu.VMEM((2, 2, rows, 128), bf16),
            pltpu.VMEM((2, 2, rows, 384), bf16),
            pltpu.VMEM((2, 2, rows, 256), bf16),
            pltpu.VMEM((2, 2, rows, 256), bf16),
            pltpu.VMEM((2, 2, rows, 128), bf16),
            pltpu.VMEM((2, rows, 256), bf16),
            pltpu.VMEM((2, rows, 128), bf16),
            pltpu.VMEM((2, rows, 384), bf16),
            pltpu.VMEM((2, rows, 256), bf16),
            pltpu.VMEM((2, rows, 256), bf16),
            pltpu.VMEM((2, rows, 128), bf16),
            pltpu.VMEM((2, rows, 384), bf16),
            pltpu.VMEM((2, rows, 256), bf16),
            pltpu.VMEM((VROWS, 128), f32),
            pltpu.VMEM((4, VROWS, 128), f32),
            pltpu.VMEM((6, VROWS, 128), f32),
            sem((NK,)),
            sem((NK + 1,)),
            sem((NK + 1,)),
            sem((NK + 1, 2, 3)),
            sem((NK + 1, 2, 3)),
            sem((NK + 1, NZ)),
            sem((NK + 1, NZ)),
            sem((12,)),
            sem((12,)),
            sem((NK,)),
            sem((NK,)),
            sem((NK, NZ)),
            sem((NK, 5)),
            sem((NK,)),
            sem((NK,)),
            sem((2, 2, 4)),
            sem((2, 2, 4)),
            sem((6,)),
            sem((6,)),
        ],
        compiler_params=pltpu.CompilerParams(
            collective_id=0, has_side_effects=True, vmem_limit_bytes=58 << 20
        ),
        cost_estimate=pl.CostEstimate(
            flops=20 * 2**30, bytes_accessed=8 * 2**20, transcendentals=2**21
        ),
    )(
        bucket_ids,
        residue_counts.reshape(SLOTS),
        residual_in,
        cotangent,
        ln_gain.reshape(1, width),
        ln_bias.reshape(1, width),
        b_back.reshape(1, width),
        jnp.asarray(cos),
        jnp.asarray(sin),
        b_in.reshape(1, 128),
        w_qkv,
        w_out.T,
        w_in,
        w_back.T,
    )
    held = [pltpu.with_memory_space_constraint(v, pltpu.VMEM) for v in held]
    outs = pl.pallas_call(
        write_kernel,
        out_shape=shapes,
        in_specs=[vm] * 10,
        out_specs=(anyspace,) * 10,
        scratch_shapes=[sem((10,))],
    )(*held)
    block_out, grad_input, grad_w_qkv, gwo, grad_w_in, gwb, lng, lnb, bbk, gbin = outs
    return (
        block_out,
        grad_input,
        lng.reshape(32),
        lnb.reshape(32),
        grad_w_qkv,
        gwo.T,
        grad_w_in,
        gbin.reshape(128),
        gwb.T,
        bbk.reshape(32),
    )


def solution(mesh):
    placed = (
        P(("dp", "mp"), None),
        P(("dp", "mp"), None),
        P(),
        P(),
        P(None, "dp", "mp"),
        P("mp", "dp"),
        P("dp", "mp"),
        P(("mp", "dp")),
        P("mp", "dp"),
        P(),
        P("dp"),
        P("dp", None),
    )
    return jax.shard_map(
        on_quad if fits_quad(mesh) else on_device,
        mesh=mesh,
        in_specs=placed,
        out_specs=(
            P(("dp", "mp"), None),
            P(("dp", "mp"), None),
            P(("dp", "mp")),
            P(("dp", "mp")),
            P(None, "dp", "mp"),
            P("mp", "dp"),
            P("dp", "mp"),
            P(("mp", "dp")),
            P("mp", "dp"),
            P(("dp", "mp")),
        ),
        check_vma=False,
    )
```

profile of v0, /device:TPU:0, one launch (start us, length us, event | category | flops | bytes accessed | tf_op | source)
XLA Modules:
  0.0 126.5 jit_solution(10669197147735306075)
XLA Ops:
  1.3 123.5 %shard_map.213 = (bf16[256,1024]{1,0:T(8,128)(2,1)S(1)}, bf16[256,1024]{1,0:T(8,128)(2,1)S(1)}, f32[3,64,512]{2,1,0:T(8,128)S(1)}, f32[64,512]{1,0:T(8,128)S(1)}...) custom-call(s32[1]{0:T(128)S(6)} %copy.24.bucket_ref, ...), custom_call_target="tpu_custom_call" | custom-call | flops 21474836480 | bytes 8388608 | tf_op jit(solution)/shard_map/pallas_call | solution.py:1144
  124.8 1.6 %shard_map.214 = (bf16[256,1024]{1,0:T(8,128)(2,1)}, bf16[256,1024]{1,0:T(8,128)(2,1)}, f32[3,64,512]{2,1,0:T(8,128)}, f32[64,512]{1,0:T(8,128)}, f32[64,2048]{1...) custom-call(bf16[256,1024]{1,0:T(8,128)(2,1)S(1)} %get-tuple-element, ...), custom_call_target="tpu_custom_call" | custom-call | tf_op jit(solution)/shard_map/pallas_call | solution.py:1237
where the time goes:
time: 127 us
  Pallas kernels  125 us (98%)
  between operations  1.46 us (1%)
    pallas_call x1, Pallas kernels, on_quad(): pl.pallas_call(layer_kernel, out_shape=tuple((pltpu.VMEM(v.shape, v.dtype...  123 us

commit v1 on v0

--- a/solution.py
+++ b/solution.py
@@ -345,6 +345,7 @@
     KR,
     VR,
     R,
+    SL,
     XV,
     CV,
     COSV,
@@ -679,6 +680,7 @@
         put(k, 1 - y, YR[k].astype(f32))
 
     rturns = iter(range(NK + 2))
+    rorder = [NQ + 1] + [k for k in range(NK) if k != NQ + 1]
 
     def rs_turn():
         r = next(rturns, None)
@@ -686,7 +688,7 @@
             return
         for s, f in enumerate((rs_hop1, rs_hop2, rs_final)):
             if 0 <= r - s < NK:
-                f(r - s)
+                f(rorder[r - s])
 
     def rs_sent(k):
         rs_c(k).wait_send()
@@ -883,28 +885,30 @@
     def slice_of(j):
         return NQ + 2 * j, NQ + 1 + 2 * j
 
-    def feed(j, m, count=1):
+    def all_rows(ref):
+        return ref[...].reshape(4 * rows, width)
+
+    def feed(j):
         ki, kb = slice_of(j)
-        n = count * rows
         b0 = B[2 * y + lax.div(j, 2), lax.rem(j, 2), 0].astype(f32)[0:1, :]
         b1 = B[2 * y + lax.div(j, 2), lax.rem(j, 2), 1].astype(f32)[0:1, :]
-        take = lambda ref: ref[pl.ds(m, count)].reshape(n, width)
-        u = dot_nn(take(NA), weight(ki)) + jnp.concatenate([b0, b1], axis=1)
+        u = dot_nn(all_rows(NA), weight(ki)) + jnp.concatenate([b0, b1], axis=1)
         u2 = u * u
         k0 = float(np.sqrt(2.0 / np.pi))
         t = jnp.tanh(k0 * u * (1.0 + 0.044715 * u2))
-        act = (0.5 * u * (1.0 + t)).astype(bf16)
-        slope = 0.5 * (1.0 + t) + (0.5 * k0) * u * (1.0 - t * t) * (1.0 + 0.134145 * u2)
-        hg = (dot_nn(take(SA), weight(kb)) * slope).astype(bf16)
-        rs = pl.ds(pl.multiple_of(m * rows, rows), n)
-        R[kb, rs, :] = act
-        R[ki, rs, :] = hg
-        OUT[pl.ds(m, count)] += dot_nt(act, weight(kb)).reshape(count, rows, width)
-        DN[pl.ds(m, count)] += dot_nt(hg, weight(ki)).reshape(count, rows, width)
+        R[kb] = (0.5 * u * (1.0 + t)).astype(bf16)
+        SL[...] = 0.5 * (1.0 + t) + (0.5 * k0) * u * (1.0 - t * t) * (1.0 + 0.134145 * u2)
+
+    def feed_back(j):
+        ki, kb = slice_of(j)
+        hg = (dot_nn(all_rows(SA), weight(kb)) * SL[...]).astype(bf16)
+        R[ki] = hg
+        OUT[...] += dot_nt(R[kb], weight(kb)).reshape(4, rows, width)
+        DN[...] += dot_nt(hg, weight(ki)).reshape(4, rows, width)
         at = 24 + x * 16 + y * 8 + 2 * j
         total = jnp.sum(hg.astype(f32), axis=0, keepdims=True)
-        V[pl.ds(at, 1), :] += total[:, :128]
-        V[pl.ds(at + 1, 1), :] += total[:, 128:]
+        V[pl.ds(at, 1), :] = total[:, :128]
+        V[pl.ds(at + 1, 1), :] = total[:, 128:]
 
     def feed_grads(j):
         lax.fori_loop(0, 2, lambda i, _: (grad_of(NQ + 2 * j + i, i), 0)[1], 0)
@@ -956,12 +960,22 @@
 
         @pl.when(i == 3)
         def _():
+            g_far(1)
+            grad_of(NQ + 1, 1)
+
+        attend(near(i))
+
+        @pl.when(i == 2)
+        def _():
             g_far(0)
             project(m_d)
-            g_far(1)
-
-        attend(near(i))
-        late_turn(8 + i)
+            arrived(NQ)
+            feed(0)
+
+        @pl.when(i < 3)
+        def _():
+            late_turn(8 + i)
+
         return 0
 
     lax.fori_loop(0, 4, rows_turn, 0)
@@ -969,18 +983,28 @@
     def head_grads(k, _):
         grad_of(k, lax.div(k, 3))
 
+        @pl.when(k == 1)
+        def _():
+            late_turn(11)
+
         @pl.when(k > 0)
         def _():
             rs_begin(k - 1)
 
         return 0
 
+    rs_begin(NQ + 1)
     lax.fori_loop(0, NQ, head_grads, 0)
     ag_turn()
 
     def slices(j, _):
-        arrived(NQ + 2 * j, NQ + 1 + 2 * j)
-        feed(j, 0, 4)
+        @pl.when(j > 0)
+        def _():
+            arrived(NQ + 2 * j)
+            feed(j)
+
+        arrived(NQ + 1 + 2 * j)
+        feed_back(j)
 
         @pl.when(j == 0)
         def _():
@@ -991,13 +1015,12 @@
         @pl.when(j == 1)
         def _():
             ag_turn()
-            feed_grads(0)
+            grad_of(NQ, 0)
             rs_turn()
-            rs_begin(4)
+            rs_begin(NQ)
 
         @pl.when(j == 2)
         def _():
-            rs_begin(5)
             ag_turn()
             rs_turn()
 
@@ -1017,14 +1040,13 @@
     rs_begin(9)
     rs_turn()
     e_second(1, 0, DN)
-    e_first(0, 0, OUT)
     feed_grads(3)
     rs_begin(10)
     rs_begin(11)
+    rs_turn()
     e_second(1, 1, DN)
+    e_first(0, 0, OUT)
     e_first_y(0, 1, OUT)
-    rs_turn()
-    rs_turn()
     rs_turn()
     rs_turn()
     for u in range(2):
@@ -1043,20 +1065,20 @@
     mex = jnp.mean(e * xhat, axis=-1, keepdims=True)
     gin_ref[...] = (SA[m_own].astype(f32) + RSTD[:, 0:1] * (e - me - xhat * mex)).astype(bf16)
     v_step(0)
+    rs_turn()
     e_first_x(0, 1, OUT)
+    rs_turn()
+    v_step(1)
     e_second(0, 0, OUT)
     rs_turn()
-    v_step(1)
+    v_step(2)
     rs_turn()
-    v_step(2)
-    for k in range(6):
+    e_second(0, 1, OUT)
+    for k in rorder[:9]:
         rs_out(k)
     rs_turn()
-    e_second(0, 1, OUT)
-    rs_turn()
-    for k in range(6, 9):
-        rs_out(k)
-    for k in range(9, NK):
+    rs_out(rorder[9])
+    for k in rorder[10:]:
         rs_out(k)
     for i in range(3):
         v_copy(3 + i, dev_z[i]).wait_recv()
@@ -1157,6 +1179,7 @@
             pltpu.VMEM((4, rows, TILE), bf16),
             pltpu.VMEM((4, rows, TILE), bf16),
             pltpu.VMEM((NK, 4 * rows, TILE), bf16),
+            pltpu.VMEM((4 * rows, TILE), f32),
             pltpu.VMEM((rows, width), bf16),
             pltpu.VMEM((rows, width), bf16),
             pltpu.VMEM((rows, 128), f32),

time: 127 us -> 126 us (level)
  no operation moved by 1% of the time
where the time goes in v1:
time: 126 us
  Pallas kernels  124 us (98%)
  between operations  1.46 us (1%)
    pallas_call x1, Pallas kernels, on_quad(): pl.pallas_call(layer_kernel, out_shape=tuple((pltpu.VMEM(v.shape, v.dtype...  122 us

profile of v1, /device:TPU:0, one launch (start us, length us, event | category | flops | bytes accessed | tf_op | source)
XLA Modules:
  0.0 125.5 jit_solution(4404590679416740574)
XLA Ops:
  1.3 122.5 %shard_map.213 = (bf16[256,1024]{1,0:T(8,128)(2,1)S(1)}, bf16[256,1024]{1,0:T(8,128)(2,1)S(1)}, f32[3,64,512]{2,1,0:T(8,128)S(1)}, f32[64,512]{1,0:T(8,128)S(1)}...) custom-call(s32[1]{0:T(128)S(6)} %copy.24.bucket_ref, ...), custom_call_target="tpu_custom_call" | custom-call | flops 21474836480 | bytes 8388608 | tf_op jit(solution)/shard_map/pallas_call | solution.py:1166
  123.8 1.6 %shard_map.214 = (bf16[256,1024]{1,0:T(8,128)(2,1)}, bf16[256,1024]{1,0:T(8,128)(2,1)}, f32[3,64,512]{2,1,0:T(8,128)}, f32[64,512]{1,0:T(8,128)}, f32[64,2048]{1...) custom-call(bf16[256,1024]{1,0:T(8,128)(2,1)S(1)} %get-tuple-element, ...), custom_call_target="tpu_custom_call" | custom-call | tf_op jit(solution)/shard_map/pallas_call | solution.py:1260

commit v2 on v1

--- a/solution.py
+++ b/solution.py
@@ -962,13 +962,14 @@
         def _():
             g_far(1)
             grad_of(NQ + 1, 1)
+            project(m_d)
+            rs_begin(NQ + 1)
 
         attend(near(i))
 
         @pl.when(i == 2)
         def _():
             g_far(0)
-            project(m_d)
             arrived(NQ)
             feed(0)
 
@@ -993,7 +994,6 @@
 
         return 0
 
-    rs_begin(NQ + 1)
     lax.fori_loop(0, NQ, head_grads, 0)
     ag_turn()
 
@@ -1015,9 +1015,7 @@
         @pl.when(j == 1)
         def _():
             ag_turn()
-            grad_of(NQ, 0)
             rs_turn()
-            rs_begin(NQ)
 
         @pl.when(j == 2)
         def _():
@@ -1030,7 +1028,9 @@
 
     for u in range(2):
         e_first(1, u, DN)
+    grad_of(NQ, 0)
     rs_turn()
+    rs_begin(NQ)
     feed_grads(1)
     rs_begin(6)
     rs_begin(7)

time: 126 us -> 124 us (0.984)
  Pallas kernels: 124 us -> 122 us
    pallas_call x1, Pallas kernels: 122 us -> 121 us  [on_quad(): pl.pallas_call(layer_kernel, out_shape=tuple((pltpu.VMEM(v.shape, v.dtype...]
where the time goes in v2:
time: 124 us
  Pallas kernels  122 us (98%)
  between operations  1.46 us (1%)
    pallas_call x1, Pallas kernels, on_quad(): pl.pallas_call(layer_kernel, out_shape=tuple((pltpu.VMEM(v.shape, v.dtype...  121 us

profile of v2, /device:TPU:0, one launch (start us, length us, event | category | flops | bytes accessed | tf_op | source)
XLA Modules:
  0.0 123.9 jit_solution(3626271712534500353)
XLA Ops:
  1.3 120.9 %shard_map.213 = (bf16[256,1024]{1,0:T(8,128)(2,1)S(1)}, bf16[256,1024]{1,0:T(8,128)(2,1)S(1)}, f32[3,64,512]{2,1,0:T(8,128)S(1)}, f32[64,512]{1,0:T(8,128)S(1)}...) custom-call(s32[1]{0:T(128)S(6)} %copy.24.bucket_ref, ...), custom_call_target="tpu_custom_call" | custom-call | flops 21474836480 | bytes 8388608 | tf_op jit(solution)/shard_map/pallas_call | solution.py:1166
  122.2 1.6 %shard_map.214 = (bf16[256,1024]{1,0:T(8,128)(2,1)}, bf16[256,1024]{1,0:T(8,128)(2,1)}, f32[3,64,512]{2,1,0:T(8,128)}, f32[64,512]{1,0:T(8,128)}, f32[64,2048]{1...) custom-call(bf16[256,1024]{1,0:T(8,128)(2,1)S(1)} %get-tuple-element, ...), custom_call_target="tpu_custom_call" | custom-call | tf_op jit(solution)/shard_map/pallas_call | solution.py:1260

commit v3 on v2

--- a/solution.py
+++ b/solution.py
@@ -554,7 +554,7 @@
         for s in range(NZ - 1):
             ag_step(t - 2 - s, s)
 
-    P0 = 80
+    P0 = 96
     parts = (pl.ds(0, P0), pl.ds(P0, rows - P0))
     BUF = (NA, SA)
 
@@ -791,9 +791,11 @@
     for i in range(8):
         V[16 + i : 17 + i, :] = back_sum[:, i * 128 : (i + 1) * 128]
     pl.semaphore_wait(barrier, len(peers))
-    for k in order:
+    for k in order[:6]:
         y_copy(k).start()
     g_send(0)
+    for k in order[6:]:
+        y_copy(k).start()
     g_send(1)
     ag_turn()
     ag_turn()

time: 124 us -> 123 us (level)
    pallas_call x1, Pallas kernels: 121 us -> 119 us  [on_quad(): pl.pallas_call(layer_kernel, out_shape=tuple((pltpu.VMEM(v.shape, v.dtype...]
where the time goes in v3:
time: 123 us
  Pallas kernels  121 us (98%)
  between operations  1.46 us (1%)
    pallas_call x1, Pallas kernels, on_quad(): pl.pallas_call(layer_kernel, out_shape=tuple((pltpu.VMEM(v.shape, v.dtype...  119 us

profile of v3, /device:TPU:0, one launch (start us, length us, event | category | flops | bytes accessed | tf_op | source)
XLA Modules:
  0.0 122.5 jit_solution(15399549589137268615)
XLA Ops:
  1.3 119.5 %shard_map.213 = (bf16[256,1024]{1,0:T(8,128)(2,1)S(1)}, bf16[256,1024]{1,0:T(8,128)(2,1)S(1)}, f32[3,64,512]{2,1,0:T(8,128)S(1)}, f32[64,512]{1,0:T(8,128)S(1)}...) custom-call(s32[1]{0:T(128)S(6)} %copy.24.bucket_ref, ...), custom_call_target="tpu_custom_call" | custom-call | flops 21474836480 | bytes 8388608 | tf_op jit(solution)/shard_map/pallas_call | solution.py:1168
  120.8 1.6 %shard_map.214 = (bf16[256,1024]{1,0:T(8,128)(2,1)}, bf16[256,1024]{1,0:T(8,128)(2,1)}, f32[3,64,512]{2,1,0:T(8,128)}, f32[64,512]{1,0:T(8,128)}, f32[64,2048]{1...) custom-call(bf16[256,1024]{1,0:T(8,128)(2,1)S(1)} %get-tuple-element, ...), custom_call_target="tpu_custom_call" | custom-call | tf_op jit(solution)/shard_map/pallas_call | solution.py:1262

commit v4 on v3

--- a/solution.py
+++ b/solution.py
@@ -794,9 +794,14 @@
     for k in order[:6]:
         y_copy(k).start()
     g_send(0)
-    for k in order[6:]:
+    g_copy(1, 0, 0, m_own).start()
+    g_copy(1, 1, 0, m_own).start()
+    for k in order[6:9]:
         y_copy(k).start()
-    g_send(1)
+    g_copy(1, 1, 1, m_own).start()
+    for k in order[9:]:
+        y_copy(k).start()
+    g_copy(1, 0, 1, m_own).start()
     ag_turn()
     ag_turn()
 

time: 123 us -> 123 us (level)
  no operation moved by 1% of the time
where the time goes in v4:
time: 123 us
  Pallas kernels  121 us (98%)
  between operations  1.46 us (1%)
    pallas_call x1, Pallas kernels, on_quad(): pl.pallas_call(layer_kernel, out_shape=tuple((pltpu.VMEM(v.shape, v.dtype...  119 us

profile of v4, /device:TPU:0, one launch (start us, length us, event | category | flops | bytes accessed | tf_op | source)
XLA Modules:
  0.0 122.5 jit_solution(13027425888616132443)
XLA Ops:
  1.3 119.5 %shard_map.213 = (bf16[256,1024]{1,0:T(8,128)(2,1)S(1)}, bf16[256,1024]{1,0:T(8,128)(2,1)S(1)}, f32[3,64,512]{2,1,0:T(8,128)S(1)}, f32[64,512]{1,0:T(8,128)S(1)}...) custom-call(s32[1]{0:T(128)S(6)} %copy.24.bucket_ref, ...), custom_call_target="tpu_custom_call" | custom-call | flops 21474836480 | bytes 8388608 | tf_op jit(solution)/shard_map/pallas_call | solution.py:1173
  120.8 1.6 %shard_map.214 = (bf16[256,1024]{1,0:T(8,128)(2,1)}, bf16[256,1024]{1,0:T(8,128)(2,1)}, f32[3,64,512]{2,1,0:T(8,128)}, f32[64,512]{1,0:T(8,128)}, f32[64,2048]{1...) custom-call(bf16[256,1024]{1,0:T(8,128)(2,1)S(1)} %get-tuple-element, ...), custom_call_target="tpu_custom_call" | custom-call | tf_op jit(solution)/shard_map/pallas_call | solution.py:1267
